TPU v7x, 32 devices: a whole 2x2x4 slice. The times are simulated.
32 devices in a mesh: seq: 32 (over z, y, x, core), head: 1.
Axes of the slice: x: 2, y: 2, z: 4, core: 2. Of those that a mesh axis runs over, the one named last changes fastest.
Arguments:
- x_in: bfloat16 [16384, 4096], P('seq', 'head'), may hold values from -6 to 6
- gate_input: bfloat16 [16384, 4096], P('seq', 'head'), may hold values from -6 to 6
- in_b: bfloat16 [16384, 512], P('seq', 'head'), may hold values from -2 to 2
- in_c: bfloat16 [16384, 512], P('seq', 'head'), may hold values from -2 to 2
- step_size: float32 [16384, 64], P('seq', 'head'), may hold values from 0.02 to 0.2
- log_decay: float32 [16384, 64], P('seq', 'head'), may hold values from -0.7 to 0, as said below
- skip_gain: float32 [64], P('head'), may hold values from 0.5 to 1.5
- norm_gain: float32 [4096], P('head'), may hold values from 0.5 to 1.5
- out_weight: bfloat16 [4096, 8192], P('head', 'seq'), may hold values from -0.046875 to 0.046875
- probe: bfloat16 [32, 8192, 128], P('seq', 'head'), may hold values from -0.29882812 to 0.29882812
- span_start: int32 [2048], P('seq'), may hold values from 0 to 16383, as said below
- span_len: int32 [2048], P('seq'), may hold values from 1 to 128, as said below
- span_owner: int32 [2048, 1], P('seq'), may hold values from 0 to 31; in each aligned block of 64 rows (0 to 63, 64 to 127, ...) at most 2 rows name the same one
- span_label: int32 [2048], P('seq'), may hold values from 0 to 127
Outputs:
- layer_out: bfloat16 [16384, 8192], P('seq', 'head')
- probe_grad: float32 [32, 8192, 128], P('seq', 'head')
- slot_loss: float32 [32, 64], P('seq')
Inputs may be any that keep to these rules, and one draw needn't show every extreme that they name: `log_decay`: log of a decay factor in (0, 1]. Span i starts among tokens (i // 64) * 512 to (i // 64 + 1) * 512 - 1, and span_start + span_len <= 16384. `span_len`: the first span of every block of 64 spans is 128 long. `span_owner`: in each aligned block of 64 spans no owner appears more than 2 times.
All inputs are finite; a program needn't handle non-finite values.
Results may differ from a plain program's by a relative error of at most 0.0068.
Values may be sent and summed in bfloat16 or wider, within the bound.
A program may use at most 256 MiB of HBM per device.

v0:
```python
import jax
import jax.numpy as jnp
from jax import lax
from jax.sharding import PartitionSpec as P

HEAD_DIM = 64
STATE = 128
CAP = 2


def prefix(part, axis, combine, identity):
    place = lax.axis_index(axis)
    gathered = jax.tree.map(lambda a: lax.all_gather(a, axis), part)
    state = jax.tree.map(lambda a, e: jnp.zeros_like(a) + jnp.asarray(e, a.dtype), part, identity)

    def one(step, state):
        return combine(
            state, jax.tree.map(lambda a: lax.dynamic_index_in_dim(a, step, 0, False), gathered)
        )

    return lax.fori_loop(0, place, one, state)


def from_behind(value, axis, steps):
    count = lax.axis_size(axis)
    leading, last = (max(0, -steps), min(count, count - steps))
    return lax.ppermute(value, axis, [(source, source + steps) for source in range(leading, last)])


def segment_summands(xs, bmat, cmat, dtk, cum):
    high = lax.Precision.HIGHEST
    tok = xs.shape[0]
    cb = jnp.einsum("tgn,sgn->gts", cmat, bmat, precision=high)
    ordered = jnp.transpose(cum, (1, 2, 0))
    diff = ordered[:, :, :, None] - ordered[:, :, None, :]
    lower = jnp.arange(tok)[:, None] >= jnp.arange(tok)[None, :]
    decay = jnp.where(lower, jnp.exp(jnp.where(lower, diff, 0.0)), 0.0)
    weights = cb[:, None] * decay * jnp.transpose(dtk, (1, 2, 0))[:, :, None, :]
    intra = jnp.einsum("gkts,sgkp->tgkp", weights, xs, precision=high)
    tail = jnp.exp(cum[-1][None] - cum) * dtk
    local_state = jnp.einsum("tgk,tgkp,tgn->gkpn", tail, xs, bmat, precision=high)
    return (intra, local_state, cum[-1])


def inter_term(cmat, cum, state_in):
    high = lax.Precision.HIGHEST
    return jnp.exp(cum)[..., None] * jnp.einsum("tgn,gkpn->tgkp", cmat, state_in, precision=high)


def piecewise_terms(xs, bmat, cmat, dtk, logd):
    tok = xs.shape[0]
    width = min(tok, 256)
    pieces = tok // width
    state = jnp.zeros((xs.shape[1], xs.shape[2], xs.shape[3], bmat.shape[2]), jnp.float32)
    total = jnp.zeros((xs.shape[1], xs.shape[2]), jnp.float32)
    results = []
    for piece in range(pieces):
        lower_edge = piece * width
        upper_edge = lower_edge + width
        inner_cum = jnp.cumsum(logd[lower_edge:upper_edge], axis=0)
        intra, local_state, piece_total = segment_summands(
            xs[lower_edge:upper_edge],
            bmat[lower_edge:upper_edge],
            cmat[lower_edge:upper_edge],
            dtk[lower_edge:upper_edge],
            inner_cum,
        )
        results.append(intra + inter_term(cmat[lower_edge:upper_edge], inner_cum, state))
        state = state * jnp.exp(piece_total)[..., None, None] + local_state
        total = total + piece_total
    return (jnp.concatenate(results, axis=0), state, total)


def combine_states(earlier, later):
    return (earlier[0] * jnp.exp(later[1])[..., None, None] + later[0], earlier[1] + later[1])


def inside_mask(first, length, place):
    return jnp.logical_and(
        place[None, :] >= first[:, None], place[None, :] < (first + length)[:, None]
    ).astype(jnp.bfloat16)


def on_device(
    x_in,
    gate_input,
    in_b,
    in_c,
    step_size,
    log_decay,
    skip_gain,
    norm_gain,
    out_weight,
    probe,
    span_start,
    span_len,
    span_owner,
    span_label,
):
    tok = x_in.shape[0]
    local_attention_heads = step_size.shape[1]
    groups_here = in_b.shape[1] // STATE
    per_group = local_attention_heads // groups_here
    xs = x_in.astype(jnp.float32).reshape(tok, groups_here, per_group, HEAD_DIM)
    bmat = in_b.astype(jnp.float32).reshape(tok, groups_here, STATE)
    cmat = in_c.astype(jnp.float32).reshape(tok, groups_here, STATE)
    dtk = step_size.reshape(tok, groups_here, per_group)
    logd = log_decay.reshape(tok, groups_here, per_group)
    cum = jnp.cumsum(logd, axis=0)
    intra, local_state, total = piecewise_terms(xs, bmat, cmat, dtk, logd)
    identity = (jnp.zeros_like(local_state), jnp.zeros_like(total))
    state_in, unused = prefix((local_state, total), "seq", combine_states, identity)
    ssm = (
        intra
        + inter_term(cmat, cum, state_in)
        + skip_gain.reshape(groups_here, per_group)[None, :, :, None] * xs
    )
    ssm = ssm.reshape(tok, groups_here, per_group * HEAD_DIM)
    gated = ssm * jax.nn.silu(
        gate_input.astype(jnp.float32).reshape(tok, groups_here, per_group * HEAD_DIM)
    )
    meansq = jnp.mean(gated * gated, axis=-1, keepdims=True)
    normalized_input = gated * lax.rsqrt(meansq + 1e-05)
    y_out = (normalized_input.reshape(tok, -1) * norm_gain[None, :]).astype(jnp.bfloat16)
    partial_out = jnp.dot(
        y_out,
        lax.all_gather(out_weight, "seq", axis=1, tiled=True),
        preferred_element_type=jnp.float32,
    )
    layer_out = lax.psum_scatter(
        partial_out.astype(jnp.bfloat16), "head", scatter_dimension=1, tiled=True
    )
    base = lax.axis_index("seq") * tok
    prev_start, prev_len = from_behind((span_start, span_len), "seq", 1)
    place = base + jnp.arange(tok, dtype=jnp.int32)
    spill_sums = jnp.dot(
        inside_mask(prev_start, prev_len, place), layer_out, preferred_element_type=jnp.float32
    )
    returned = from_behind(spill_sums, "seq", -1)
    sums = (
        jnp.dot(
            inside_mask(span_start, span_len, place), layer_out, preferred_element_type=jnp.float32
        )
        + returned
    )
    count = span_start.shape[0]
    owners = lax.axis_size("seq")
    slots_total = owners * CAP
    owner = span_owner[:, 0]
    index = jnp.arange(count)
    earlier = index[None, :] < index[:, None]
    same = owner[:, None] == owner[None, :]
    slot = jnp.sum(jnp.logical_and(same, earlier), axis=1)
    target_labels = owner * CAP + slot
    pick = jnp.arange(slots_total, dtype=jnp.int32)[:, None] == target_labels[None, :]
    send_sums = jnp.dot(pick.astype(jnp.float32), sums, precision=lax.Precision.HIGHEST).reshape(
        owners, CAP, -1
    )
    label_slots = jnp.sum(jnp.where(pick, span_label[None, :] + 1, 0), axis=1) - 1
    length_slots = jnp.sum(jnp.where(pick, span_len[None, :], 0), axis=1)
    meta = jnp.stack([label_slots, length_slots], axis=-1).reshape(owners, CAP, 2)
    got_sums, got_meta = (
        lax.all_to_all(send_sums, "seq", split_axis=0, concat_axis=0, tiled=True),
        lax.all_to_all(meta, "seq", split_axis=0, concat_axis=0, tiled=True),
    )
    labels = got_meta[:, :, 0].reshape(-1)
    lengths = got_meta[:, :, 1].reshape(-1)
    valid = labels >= 0
    feature = (
        got_sums.reshape(slots_total, -1) / jnp.maximum(lengths, 1)[:, None].astype(jnp.float32)
    ).astype(jnp.bfloat16)
    partial_logits = jnp.dot(feature, probe[0], preferred_element_type=jnp.float32)
    logits = lax.psum(partial_logits, "head")
    top = jnp.max(logits, axis=1, keepdims=True)
    lse = top[:, 0] + jnp.log(jnp.sum(jnp.exp(logits - top), axis=1))
    onehot = jnp.arange(logits.shape[1])[None, :] == labels[:, None]
    picked = jnp.sum(jnp.where(onehot, logits, 0.0), axis=1)
    loss = jnp.where(valid, lse - picked, 0.0)
    probs = jnp.exp(logits - lse[:, None])
    resid = jnp.where(valid[:, None], probs - onehot.astype(jnp.float32), 0.0).astype(jnp.bfloat16)
    grad = jnp.dot(feature.T, resid, preferred_element_type=jnp.float32)
    return (layer_out, grad[None], loss[None])


def solution(mesh):
    placed = (
        P("seq", "head"),
        P("seq", "head"),
        P("seq", "head"),
        P("seq", "head"),
        P("seq", "head"),
        P("seq", "head"),
        P("head"),
        P("head"),
        P("head", "seq"),
        P("seq", "head", None),
        P("seq"),
        P("seq"),
        P("seq", None),
        P("seq"),
    )
    return jax.shard_map(
        on_device,
        mesh=mesh,
        in_specs=placed,
        out_specs=(P("seq", "head"), P("seq", "head", None), P("seq", None)),
        check_vma=False,
    )
```

profile of v0, /device:TPU:0, one launch (start us, length us, event | category | flops | bytes accessed | tf_op | source)
XLA Modules:
  0.0 933.1 jit_solution(3031816082864726548)
XLA Ops:
  7.2 1.0 fusion.89
  8.3 2.3 reduce-window.24
  11.5 2.3 reduce-window.20
  14.7 1.5 fusion.90
  16.3 4.7 fusion.86
  21.0 4.1 copy.130
  25.3 0.9 slice_reduce_fusion.2
  26.3 4.1 copy.138
  30.5 0.8 exponential_multiply_fusion
  31.3 3.9 fusion.34
  35.2 1.3 copy-done.1
  36.5 3.6 multiply_add_fusion
  40.9 2.4 collective-permute-start
  43.3 5.1 collective-permute-start.1
  48.4 7.6 copy.148
  56.1 0.9 reshape.230
  57.1 0.7 fusion.87
  57.8 1.1 copy.177
  59.1 4.6 reduce-window.26
  64.0 41.1 %all_gather.13 = f32[32,4,16]{2,1,0:T(4,128)S(1)} all-gather(f32[1,4,16]{2,1,0:T(4,128)S(1)} %copy.145), channel_id=1, replica_groups=mesh['seq'=32,'head'=1] {'seq'}, dimensions={0}, use_global_device_ids=true | all-gather | bytes 8448 | tf_op jit(solution)/shard_map/all_gather | solution.py:13
  105.9 1.8 fusion.54
  107.8 1.9 fusion.48
  110.0 14.7 %fusion.27 = f32[256,4,16,64]{0,3,2,1:T(8,128)} fusion(f32[4,16,64,256]{3,2,1,0:T(8,128)S(1)} %fusion.48, bf16[256,4,16,64]{0,3,2,1:T(8,128)(2,1)S(1)} %bitcast.164, f32[4,16,256]{2,1,0:T(8,128)S(1)} %bitcast.183, f32[4,16,256]{2,1,0:T(8,128)S(1)} %copy-done.14, f32[4,256,256]{2,1,0:T(8,128)S(1)} %fusion.95, pred[256,256]{1,0:T(8,128)(4,1)S(1)} %iota_compare_fusion, ...), kind=kOutput, calls=%fused_computation.36 | convolution fusion | flops 3244294144 | bytes 11796480 | tf_op jit(solution)/shard_map/gkts,sgkp->tgkp/dot_general | solution.py:39
  124.7 14.7 %fusion.28 = f32[256,4,16,64]{0,3,2,1:T(8,128)} fusion(f32[4,16,64,256]{3,2,1,0:T(8,128)S(1)} %fusion.54, bf16[256,4,16,64]{0,3,2,1:T(8,128)(2,1)S(1)} %bitcast.162, f32[4,16,256]{2,1,0:T(8,128)S(1)} %bitcast.181, f32[4,16,256]{2,1,0:T(8,128)S(1)} %copy-done.15, f32[4,256,256]{2,1,0:T(8,128)S(1)} %fusion.94, pred[256,256]{1,0:T(8,128)(4,1)S(1)} %iota_compare_fusion, ...), kind=kOutput, calls=%fused_computation.38 | convolution fusion | flops 3244294144 | bytes 11796480 | tf_op jit(solution)/shard_map/gkts,sgkp->tgkp/dot_general | solution.py:39
  139.4 7.1 copy.150
  147.2 252.3 %all-gather.6.cloned.1.call-done = f32[128,16,64,128]{3,2,1,0:T(8,128)} async-done(((f32[4,16,64,128]{3,2,1,0:T(8,128)}), f32[128,16,64,128]{3,2,1,0:T(8,128)}) %all-gather.6.cloned.1.call-update) | async-done | bytes 67108880 | tf_op jit(solution)/shard_map/all_gather | solution.py:13
  399.5 1.6 broadcast.113
  402.1 15.1 %multiply_reduce_fusion = (f32[512,4]{0,1:T(4,128)S(1)}, f32[512,4,16,64]{0,3,2,1:T(8,128)}) fusion(f32[512,4096]{0,1:T(8,128)} %copy.150, f32[512,4,16,64]{0,3,2,1:T(8,128)} %bitcast.158, f32[4,16]{1,0:T(4,128)S(1)} %mul.167, f32[4,16,64,128]{3,2,1,0:T(8,128)} %get-tuple-element.47, bf16[512,4,128,1]{2,1,0,3:T(4,128)(2,1)S(1)} %bitcast.173, ...), kind=kOutput, calls=%fused_computation.22 | convolution fusion | flops 3246389248 | bytes 36315392 | tf_op jit(solution)/shard_map/tgn,gkpn->tgkp/dot_general | solution.py:47
  417.4 1.1 mul.175
  418.6 11.4 %copy.185 = f32[64,8,4,1024]{3,1,2,0:T(8,128)} copy(f32[64,8,4,1024]{3,2,1,0:T(4,128)S(1)} %bitcast.157) | data formatting | bytes 16777216
  430.0 9.0 copy.149
  439.0 318.0 %all-gather.4.cloned.1.call-done = bf16[4096,8192]{1,0:T(8,128)(2,1)} async-done(((bf16[4096,256]{1,0:T(8,128)(2,1)}), bf16[4096,8192]{1,0:T(8,128)(2,1)}) %all-gather.4.cloned.1.call-update) | async-done | bytes 67108880 | tf_op jit(solution)/shard_map/all_gather | solution.py:127
  757.0 60.2 %convolution_convert_fusion = bf16[512,8192]{1,0:T(8,128)(2,1)} fusion(bf16[4096,8192]{1,0:T(8,128)(2,1)} %all-gather.4.cloned.1.call-done, f32[512,4096]{1,0:T(8,128)} %bitcast.160, f32[512,4096]{1,0:T(8,128)} %copy.149, f32[4096]{0:T(1024)S(1)} %copy-done.20, bf16[512,4096]{1,0:T(8,128)(2,1)} %param.17), kind=kOutput, calls=%fused_computation.16 | convolution fusion | flops 34382807040 | bytes 96485376 | tf_op jit(solution)/shard_map/dot_general | solution.py:125
  817.2 6.4 fusion.57
  823.5 1.3 collective-permute-start.2
  825.0 0.8 select_reduce_fusion.2
  826.7 4.7 all-to-all-start.1
  832.0 5.0 fusion.61
  837.1 4.2 fusion.43
  841.3 3.5 reshape.235
  844.8 7.8 all-to-all-done.1
  852.6 10.1 %all-to-all-start = ((f32[32,2,8192]{2,1,0:T(2,128)}), f32[32,2,8192]{2,1,0:T(2,128)}, u32[]{:S(2)}, u32[]{:S(2)}) async-start(f32[32,2,8192]{2,1,0:T(2,128)} %reshape.235), calls=%async_computation | async-start | bytes 4194304 | tf_op jit(solution)/shard_map/all_to_all | solution.py:163
  863.2 48.3 %all-to-all-done = f32[32,2,8192]{2,1,0:T(2,128)} async-done(((f32[32,2,8192]{2,1,0:T(2,128)}), f32[32,2,8192]{2,1,0:T(2,128)}, u32[]{:S(2)}, u32[]{:S(2)}) %all-to-all-start) | async-done | bytes 2097184 | tf_op jit(solution)/shard_map/all_to_all | solution.py:163
  911.6 2.6 divide_convert_fusion.1
  914.2 1.2 convert_element_type.56
  915.4 1.8 fusion.91
  918.0 3.7 reshape.236
  921.6 4.4 convolution_bitcast_fusion
  (103 shorter events, 9.6 us)
Async XLA Ops:
  7.2 908.2 %copy-start = (bf16[1,8192,128]{2,1,0:T(8,128)(2,1)S(1)}, bf16[1,8192,128]{2,1,0:T(8,128)(2,1)}, u32[]{:S(2)}) copy-start(bf16[1,8192,128]{2,1,0:T(8,128)(2,1)} %param.25) | copy-start | bytes 6291460
  7.2 392.3 %all-gather.6.cloned.1.call-start = ((), (), s32[]{:S(2)}) async-start(), calls=%async_computation.3 | async-start | bytes 69206016 | tf_op jit(solution)/shard_map/all_gather | solution.py:13
  21.0 4.1 copy-start.7
  25.2 5.4 copy-start.10
  25.2 5.4 copy-start.12
  30.5 6.0 copy-start.4
  35.2 1.3 copy-start.1
  36.5 4.4 copy-start.18
  40.1 716.8 %all-gather.4.cloned.1.call-start = ((), (), s32[]{:S(2)}) async-start(), calls=%async_computation.2 | async-start | bytes 69206016 | tf_op jit(solution)/shard_map/all_gather | solution.py:127
  40.9 105.6 %collective-permute-start = (s32[64]{0:T(128)S(1)}, s32[64]{0:T(128)S(1)}, u32[]{:S(2)}, u32[]{:S(2)}) collective-permute-start(s32[64]{0:T(128)S(1)} %copy-done.18), channel_id=1, source_target_pairs={{0,1},{1,2},{2,3},{3,4},{4,5},{5,6},{6,7},{7,8},{8,9},{9,10},{10,1... | collective-permute-start | bytes 776 | tf_op jit(solution)/shard_map/ppermute | solution.py:27
  43.3 103.3 %collective-permute-start.1 = (s32[64]{0:T(128)}, s32[64]{0:T(128)}, u32[]{:S(2)}, u32[]{:S(2)}) collective-permute-start(s32[64]{0:T(128)} %param.27), channel_id=1, source_target_pairs={{0,1},{1,2},{2,3},{3,4},{4,5},{5,6},{6,7},{7,8},{8,9},{9,10},{10,1... | collective-permute-start | bytes 776 | tf_op jit(solution)/shard_map/ppermute | solution.py:27
  48.4 7.7 copy-start.6
  48.4 10.7 %copy-start.9 = (f32[512,64]{0,1:T(8,128)S(1)}, f32[512,64]{0,1:T(8,128)}, u32[]{:S(2)}) copy-start(f32[512,64]{0,1:T(8,128)} %param.21) | copy-start | bytes 393220
  64.0 43.8 %copy-start.2 = (f32[4,16,64,128]{3,2,1,0:T(8,128)S(1)}, f32[4,16,64,128]{3,2,1,0:T(8,128)}, u32[]{:S(2)}) copy-start(f32[4,16,64,128]{3,2,1,0:T(8,128)} %copy-done.1) | copy-start | bytes 6291460
  107.7 2.2 copy-start.5
  107.7 2.2 copy-start.13
  107.8 2.2 copy-start.14
  107.8 2.2 copy-start.17
  110.0 14.7 %copy-start.3 = (bf16[256,4096]{0,1:T(8,128)(2,1)S(1)}, bf16[256,4096]{0,1:T(8,128)(2,1)}, u32[]{:S(2)}) copy-start(bf16[256,4096]{0,1:T(8,128)(2,1)} %copy.130) | copy-start | bytes 6291460
  110.0 14.7 %copy-start.11 = (f32[256,64]{0,1:T(8,128)S(1)}, f32[256,64]{0,1:T(8,128)}, u32[]{:S(2)}) copy-start(f32[256,64]{0,1:T(8,128)} %get-tuple-element.83) | copy-start | bytes 196612
  110.0 14.7 %copy-start.15 = (f32[4,16,256]{2,1,0:T(8,128)S(1)}, f32[4,16,256]{2,1,0:T(8,128)}, u32[]{:S(2)}) copy-start(f32[4,16,256]{2,1,0:T(8,128)} %get-tuple-element.93) | copy-start | bytes 196612
  110.0 14.7 %copy-start.16 = (f32[256,4,16]{0,2,1:T(8,128)S(1)}, f32[256,4,16]{0,2,1:T(8,128)}, u32[]{:S(2)}) copy-start(f32[256,4,16]{0,2,1:T(8,128)} %get-tuple-element.102) | copy-start | bytes 196612
  139.3 7.1 copy-start.19
  401.1 1.0 copy-start.8
  430.0 327.0 %copy-start.20 = (f32[4096]{0:T(1024)S(1)}, f32[4096]{0:T(1024)}, u32[]{:S(2)}) copy-start(f32[4096]{0:T(1024)} %param.23) | copy-start | bytes 49156
  817.2 7.6 copy-start.22
  817.2 7.8 copy-start.21
  823.5 13.5 %collective-permute-start.2 = (f32[64,8192]{1,0:T(8,128)}, f32[64,8192]{1,0:T(8,128)}, u32[]{:S(2)}, u32[]{:S(2)}) collective-permute-start(f32[64,8192]{1,0:T(8,128)} %fusion.57), channel_id=1, source_target_pairs={{1,0},{2,1},{3,2},{4,3},{5,4},{6,5},{7,6},{8,7},{9,8},{10,9},{11,1... | collective-permute-start | bytes 6291464 | tf_op jit(solution)/shard_map/ppermute | solution.py:27
  826.7 25.9 %all-to-all-start.1 = ((s32[32,2,2]{1,2,0:T(2,128)}), s32[32,2,2]{1,2,0:T(2,128)S(1)}, u32[]{:S(2)}, u32[]{:S(2)}) async-start(s32[32,2,2]{1,2,0:T(2,128)} %copy.152), calls=%async_computation.1 | async-start | bytes 65536 | tf_op jit(solution)/shard_map/all_to_all | solution.py:164
  852.6 59.0 %all-to-all-start = ((f32[32,2,8192]{2,1,0:T(2,128)}), f32[32,2,8192]{2,1,0:T(2,128)}, u32[]{:S(2)}, u32[]{:S(2)}) async-start(f32[32,2,8192]{2,1,0:T(2,128)} %reshape.235), calls=%async_computation | async-start | bytes 4194304 | tf_op jit(solution)/shard_map/all_to_all | solution.py:163
Sparse Core Ops, SparseCore 0:
  40.3 359.1 all-gather.5
  401.0 355.9 all-gather.3
where the time goes:
time: 940 us; the launch traced here: 933 us
  waiting for transfers between devices  627 us (67%)
  matrix products  138 us (15%)
  local copies, waits for them, and re-layouts  69.4 us (7%)
  blocking collectives  41.1 us (4%)
  starting transfers between devices  23.6 us (3%)
  other arithmetic  18.3 us (2%)
  between operations  14.8 us (2%)
    all_gather x1, waiting for transfers between devices, on_device(): lax.all_gather(out_weight, 'seq', axis=1, tiled=True)  318 us
    all_gather x1, waiting for transfers between devices, prefix(): gathered = jax.tree.map(lambda a: lax.all_gather(a, axis), part)  252 us
    dot_general x1, matrix products, on_device(): jnp.dot(y_out, lax.all_gather(out_weight, 'seq', axis=1, tiled=True), pre...  60.2 us
    all_to_all x1, waiting for transfers between devices, on_device(): lax.all_to_all(send_sums, 'seq', split_axis=0, concat_axis=0, tiled=True)  48.3 us
    all_gather x1, blocking collectives, prefix(): gathered = jax.tree.map(lambda a: lax.all_gather(a, axis), part)  41.1 us
    dot_general x2, matrix products, segment_summands(): intra = jnp.einsum('gkts,sgkp->tgkp', weights, xs, precision=high)  29.3 us
    dot_general x3, matrix products, inter_term(): jnp.einsum('tgn,gkpn->tgkp', cmat, state_in, precision=high)  18.8 us
  transfers between devices with their start and end apart: 7, of which 4 were waited for; matrix products, arithmetic and copies ran while one was open for 12% of the time, Pallas kernels for 0%

commit v1 on v0

v1 whole, which is shorter than its diff:
```python
import functools

import jax
import jax.numpy as jnp
from jax import lax
from jax.experimental import pallas as pl
from jax.experimental.pallas import tpu as pltpu
from jax.sharding import PartitionSpec as P

HEAD_DIM = 64
STATE = 128
CAP = 2
CHUNK = 128
PAIR = 2 * HEAD_DIM
META = 16
F32 = jnp.float32
BF16 = jnp.bfloat16


def from_behind(value, axis, steps):
    count = lax.axis_size(axis)
    leading, last = (max(0, -steps), min(count, count - steps))
    return lax.ppermute(value, axis, [(source, source + steps) for source in range(leading, last)])


def inside_mask(first, length, place):
    return jnp.logical_and(
        place[None, :] >= first[:, None], place[None, :] < (first + length)[:, None]
    ).astype(BF16)


def pair_of(cols, p, rows):
    low = lax.broadcasted_iota(jnp.int32, (rows, PAIR), 1) < HEAD_DIM
    a = jnp.broadcast_to(cols[:, 2 * p : 2 * p + 1], (rows, PAIR))
    b = jnp.broadcast_to(cols[:, 2 * p + 1 : 2 * p + 2], (rows, PAIR))
    return jnp.where(low, a, b)


def local_kernel(pairs, x_ref, b_ref, tail_ref, meta_ref, out_ref):
    rows = x_ref.shape[0]
    tail = tail_ref[0]
    scaled = [
        (x_ref[:, PAIR * p : PAIR * (p + 1)].astype(F32) * pair_of(tail, p, rows)).astype(BF16)
        for p in range(pairs)
    ]
    state = lax.dot_general(
        b_ref[...],
        jnp.concatenate(scaled, axis=1),
        (((0,), (0,)), ((), ())),
        preferred_element_type=F32,
    )
    for p in range(pairs):
        out_ref[p, :STATE, :] = state[:, PAIR * p : PAIR * (p + 1)].astype(BF16)
        out_ref[p, STATE:, :] = meta_ref[p]


def local_states(x_in, in_b, tail, meta, groups, pairs):
    tok = x_in.shape[0]
    width = pairs * PAIR
    return pl.pallas_call(
        functools.partial(local_kernel, pairs),
        grid=(groups,),
        in_specs=[
            pl.BlockSpec((tok, width), lambda g: (0, g)),
            pl.BlockSpec((tok, STATE), lambda g: (0, g)),
            pl.BlockSpec((1, tok, 2 * pairs), lambda g: (g, 0, 0)),
            pl.BlockSpec((pairs, META, PAIR), lambda g: (g, 0, 0)),
        ],
        out_specs=pl.BlockSpec((pairs, STATE + META, PAIR), lambda g: (g, 0, 0)),
        out_shape=jax.ShapeDtypeStruct((groups * pairs, STATE + META, PAIR), BF16),
        name="local_states",
        compiler_params=pltpu.CompilerParams(vmem_limit_bytes=40 * 2**20),
    )(x_in, in_b, tail, meta)


def prefix_kernel(per, got_ref, out_ref):
    count = got_ref.shape[0] // per
    for q in range(per):
        state = jnp.zeros((STATE, PAIR), F32)
        for k in range(count):
            out_ref[k * per + q] = state.astype(BF16)
            block = got_ref[k * per + q].astype(F32)
            keep = jnp.exp(block[STATE : STATE + 1] + block[STATE + 1 : STATE + 2])
            state = state * keep + block[:STATE]


def prefix_states(got, per):
    return pl.pallas_call(
        functools.partial(prefix_kernel, per),
        out_shape=jax.ShapeDtypeStruct((got.shape[0], STATE, PAIR), BF16),
        name="prefix_states",
        compiler_params=pltpu.CompilerParams(vmem_limit_bytes=40 * 2**20),
    )(got)


def mixer_kernel(
    pairs,
    x_ref,
    gate_ref,
    b_ref,
    c_ref,
    cum_ref,
    cumt_ref,
    dt_ref,
    skip_ref,
    gain_ref,
    in_ref,
    y_ref,
    state,
    gated,
):
    rows = x_ref.shape[0]

    @pl.when(pl.program_id(1) == 0)
    def _():
        state[...] = in_ref[...].astype(F32)

    bmat, cmat = b_ref[...], c_ref[...]
    cb = lax.dot_general(cmat, bmat, (((1,), (1,)), ((), ())), preferred_element_type=F32)
    row = lax.broadcasted_iota(jnp.int32, (rows, rows), 0)
    col = lax.broadcasted_iota(jnp.int32, (rows, rows), 1)
    cb = jnp.where(row >= col, cb, 0.0)
    low = lax.broadcasted_iota(jnp.int32, (rows, PAIR), 1) < HEAD_DIM
    cum, dt, cumt = cum_ref[0], dt_ref[0], cumt_ref[...]
    square = jnp.zeros((rows, 1), F32)
    for p in range(pairs):
        lanes = slice(PAIR * p, PAIR * (p + 1))
        x = x_ref[:, lanes].astype(F32)
        left = jnp.broadcast_to(cum[:, 2 * p : 2 * p + 1], (rows, PAIR))
        right = jnp.broadcast_to(cum[:, 2 * p + 1 : 2 * p + 2], (rows, PAIR))
        w0 = cb * jnp.exp(jnp.minimum(left - cumt[2 * p : 2 * p + 1, :], 0.0))
        w1 = cb * jnp.exp(jnp.minimum(right - cumt[2 * p + 1 : 2 * p + 2, :], 0.0))
        both = jnp.where(low, left, right)
        last = both[rows - 1 : rows, :]
        stepped = x * pair_of(dt, p, rows)
        stacked = jnp.concatenate(
            [jnp.where(low, stepped, 0.0), jnp.where(low, 0.0, stepped)], axis=0
        ).astype(BF16)
        weights = jnp.concatenate([w0, w1], axis=1).astype(BF16)
        held = state[p]
        result = jnp.dot(weights, stacked, preferred_element_type=F32)
        result += jnp.exp(both) * jnp.dot(cmat, held.astype(BF16), preferred_element_type=F32)
        result += skip_ref[0:1, lanes] * x
        ending = (stepped * jnp.exp(last - both)).astype(BF16)
        state[p] = held * jnp.exp(last) + lax.dot_general(
            bmat, ending, (((0,), (0,)), ((), ())), preferred_element_type=F32
        )
        g = gate_ref[:, lanes].astype(F32)
        u = result * (g / (1.0 + jnp.exp(-g)))
        gated[:, lanes] = u
        square += jnp.sum(u * u, axis=1, keepdims=True)
    scale = lax.rsqrt(square * (1.0 / (pairs * PAIR)) + 1e-05)
    y_ref[...] = (gated[...] * scale * gain_ref[0:1, :]).astype(BF16)


def mixer(x_in, gate, in_b, in_c, cum, cumt, dt, skip, gain, incoming, groups, pairs):
    tok = x_in.shape[0]
    width = pairs * PAIR
    wide = pl.BlockSpec((CHUNK, width), lambda g, c: (c, g))
    maps = pl.BlockSpec((CHUNK, STATE), lambda g, c: (c, g))
    cols = pl.BlockSpec((1, CHUNK, 2 * pairs), lambda g, c: (g, c, 0))
    line = pl.BlockSpec((1, width), lambda g, c: (0, g))
    return pl.pallas_call(
        functools.partial(mixer_kernel, pairs),
        grid=(groups, tok // CHUNK),
        in_specs=[
            wide,
            wide,
            maps,
            maps,
            cols,
            pl.BlockSpec((2 * pairs, CHUNK), lambda g, c: (g, c)),
            cols,
            line,
            line,
            pl.BlockSpec((pairs, STATE, PAIR), lambda g, c: (g, 0, 0)),
        ],
        out_specs=wide,
        out_shape=jax.ShapeDtypeStruct((tok, groups * width), BF16),
        scratch_shapes=[pltpu.VMEM((pairs, STATE, PAIR), F32), pltpu.VMEM((CHUNK, width), F32)],
        name="mixer",
        compiler_params=pltpu.CompilerParams(vmem_limit_bytes=40 * 2**20),
    )(x_in, gate, in_b, in_c, cum, cumt, dt, skip, gain, incoming)


def on_device(
    x_in,
    gate_input,
    in_b,
    in_c,
    step_size,
    log_decay,
    skip_gain,
    norm_gain,
    out_weight,
    probe,
    span_start,
    span_len,
    span_owner,
    span_label,
):
    tok, inner = x_in.shape
    heads = step_size.shape[1]
    groups = in_b.shape[1] // STATE
    pairs = heads // groups // 2
    owners = lax.axis_size("seq")
    weight = lax.all_gather(out_weight, "seq", axis=1, tiled=True)

    high = lax.Precision.HIGHEST
    lower = jnp.tril(jnp.ones((CHUNK, CHUNK), F32))
    cum = jnp.einsum("ts,csh->cth", lower, log_decay.reshape(-1, CHUNK, heads), precision=high)
    ends = cum[:, -1, :]
    total = jnp.sum(ends, axis=0)
    chunks = tok // CHUNK
    behind = jnp.stack(
        [sum((ends[j] for j in range(c + 1, chunks)), jnp.zeros_like(total)) for c in range(chunks)]
    )
    tail = jnp.exp(ends[:, None] - cum + behind[:, None]).reshape(tok, heads) * step_size
    cum = cum.reshape(tok, heads)

    def by_group(a):
        return jnp.transpose(a.reshape(tok, groups, 2 * pairs), (1, 0, 2))

    total_high = lax.reduce_precision(total, 8, 7)
    total_low = total - total_high
    halves = jnp.stack([total_high, total_low])
    wide = jnp.repeat(halves.reshape(2, heads // 2, 2), HEAD_DIM, axis=2)
    meta = jnp.pad(jnp.transpose(wide, (1, 0, 2)), ((0, 0), (0, META - 2), (0, 0))).astype(BF16)
    local = local_states(x_in, in_b, by_group(tail), meta, groups, pairs)

    here = heads // 2
    share = -(-here // owners)
    if share * owners > here:
        local = jnp.pad(local, ((0, share * owners - here), (0, 0), (0, 0)))
    got = lax.all_to_all(local, "seq", split_axis=0, concat_axis=0, tiled=True)
    incoming = lax.all_to_all(
        prefix_states(got, share), "seq", split_axis=0, concat_axis=0, tiled=True
    )[:here]
    skip = jnp.repeat(skip_gain, HEAD_DIM)[None]
    y = mixer(
        x_in,
        gate_input,
        in_b,
        in_c,
        by_group(cum),
        cum.T,
        by_group(step_size),
        skip,
        norm_gain[None],
        incoming,
        groups,
        pairs,
    )

    base = lax.axis_index("seq") * tok
    prev_start, prev_len = from_behind((span_start, span_len), "seq", 1)
    place = base + jnp.arange(tok, dtype=jnp.int32)
    count = span_start.shape[0]
    masks = jnp.concatenate(
        [inside_mask(prev_start, prev_len, place), inside_mask(span_start, span_len, place)]
    )
    both = jnp.dot(masks, y, preferred_element_type=F32)
    returned = from_behind(both[:count].astype(BF16), "seq", -1)
    means = (both[count:] + returned.astype(F32)) / span_len[:, None].astype(F32)
    slots_total = owners * CAP
    owner = span_owner[:, 0]
    index = jnp.arange(count)
    earlier = index[None, :] < index[:, None]
    same = owner[:, None] == owner[None, :]
    slot = jnp.sum(jnp.logical_and(same, earlier), axis=1)
    pick = jnp.arange(slots_total, dtype=jnp.int32)[:, None] == (owner * CAP + slot)[None, :]
    sent = jnp.dot(pick.astype(BF16), means.astype(BF16), preferred_element_type=F32)
    labels = jnp.sum(jnp.where(pick, span_label[None, :] + 1, 0), axis=1) - 1
    got_means = lax.all_to_all(
        sent.astype(BF16).reshape(owners, CAP, -1), "seq", split_axis=0, concat_axis=0, tiled=True
    ).reshape(slots_total, -1)
    labels = lax.all_to_all(
        labels.reshape(owners, CAP), "seq", split_axis=0, concat_axis=0, tiled=True
    ).reshape(-1)
    valid = labels >= 0

    return project(jnp.concatenate([y, got_means], axis=0), weight, probe, tok, labels, valid)


def project(rows, weight, probe, tok, labels, valid):
    out = jnp.dot(rows, weight, preferred_element_type=F32)
    if lax.axis_size("head") > 1:
        layer_out = lax.psum_scatter(
            out[:tok].astype(BF16), "head", scatter_dimension=1, tiled=True
        )
        feature = lax.psum_scatter(out[tok:], "head", scatter_dimension=1, tiled=True)
        feature = feature.astype(BF16)
    else:
        out = out.astype(BF16)
        layer_out, feature = out[:tok], out[tok:]
    logits = jnp.dot(feature, probe[0], preferred_element_type=F32)
    logits = lax.psum(logits, "head")
    top = jnp.max(logits, axis=1, keepdims=True)
    lse = top[:, 0] + jnp.log(jnp.sum(jnp.exp(logits - top), axis=1))
    onehot = jnp.arange(logits.shape[1])[None, :] == labels[:, None]
    picked = jnp.sum(jnp.where(onehot, logits, 0.0), axis=1)
    loss = jnp.where(valid, lse - picked, 0.0)
    probs = jnp.exp(logits - lse[:, None])
    resid = jnp.where(valid[:, None], probs - onehot.astype(F32), 0.0).astype(BF16)
    grad = jnp.dot(feature.T, resid, preferred_element_type=F32)
    return (layer_out, grad[None], loss[None])


def solution(mesh):
    placed = (
        P("seq", "head"),
        P("seq", "head"),
        P("seq", "head"),
        P("seq", "head"),
        P("seq", "head"),
        P("seq", "head"),
        P("head"),
        P("head"),
        P("head", "seq"),
        P("seq", "head", None),
        P("seq"),
        P("seq"),
        P("seq", None),
        P("seq"),
    )
    return jax.shard_map(
        on_device,
        mesh=mesh,
        in_specs=placed,
        out_specs=(P("seq", "head"), P("seq", "head", None), P("seq", None)),
        check_vma=False,
    )
```

time: 940 us -> 505 us (0.54)
  waiting for transfers between devices: 627 us -> 283 us
  matrix products: 138 us -> 56.4 us
  Pallas kernels: 0 us -> 41.1 us
  local copies, waits for them, and re-layouts: 69.4 us -> 32.1 us
  other arithmetic: 18.3 us -> 7.7 us
    all_gather x2 -> x1, waiting for transfers between devices: 570 us -> 228 us  [on_device(): weight = lax.all_gather(out_weight, 'seq', axis=1, tiled=True)]
    dot_general x15 -> x5, matrix products: 138 us -> 56.1 us  [the longest x1 47.9 us: project(): out = jnp.dot(rows, weight, preferred_element_type=F32)]
    all_to_all x0 -> x1, blocking collectives: none -> 49.1 us  [on_device(): got = lax.all_to_all(local, 'seq', split_axis=0, concat_axis=0, tiled=True)]
    all_gather x1 -> x0, blocking collectives: 41.1 us -> none  [prefix(): gathered = jax.tree.map(lambda a: lax.all_gather(a, axis), part)]
    pallas_call x0 -> x3, Pallas kernels: none -> 41.1 us  [the longest x1 34.6 us: mixer(): pl.pallas_call(functools.partial(mixer_kernel, pairs), grid=(groups, tok...]
    reshape x6 -> x8, local copies, waits for them, and re-layouts: 24.7 us -> 4.09 us  [the longest x2 1.64 us: by_group(): return jnp.transpose(a.reshape(tok, groups, 2 * pairs), (1, 0, 2))]
    another operation x9 -> x2, other arithmetic: 9.91 us -> 0.02 us  [the longest x1 0.01 us: on_device(): jnp.stack([sum((ends[j] for j in range(c + 1, chunks)), jnp.zeros_like(to...]
    all_to_all x2 -> x3, waiting for transfers between devices: 56.2 us -> 54.4 us  [the longest x1 21.1 us: on_device(): lax.all_to_all(prefix_states(got, share), 'seq', split_axis=0, concat_axi...]
  transfers between devices with their start and end apart: 7 -> 7, of which waited for: 4 -> 4; matrix products, arithmetic and copies ran while one was open for 12% -> 4% of each run, Pallas kernels for 0% -> 8%
where the time goes in v1:
time: 505 us; the launch traced here: 504 us
  waiting for transfers between devices  283 us (56%)
  matrix products  56.4 us (11%)
  blocking collectives  49.1 us (10%)
  Pallas kernels  41.1 us (8%)
  local copies, waits for them, and re-layouts  32.1 us (6%)
  starting transfers between devices  20 us (4%)
  between operations  14.4 us (3%)
  other arithmetic  7.7 us (2%)
    all_gather x1, waiting for transfers between devices, on_device(): weight = lax.all_gather(out_weight, 'seq', axis=1, tiled=True)  228 us
    all_to_all x1, blocking collectives, on_device(): got = lax.all_to_all(local, 'seq', split_axis=0, concat_axis=0, tiled=True)  49.1 us
    dot_general x1, matrix products, project(): out = jnp.dot(rows, weight, preferred_element_type=F32)  47.9 us
    pallas_call x1, Pallas kernels, mixer(): pl.pallas_call(functools.partial(mixer_kernel, pairs), grid=(groups, tok...  34.6 us
    all_to_all x1, waiting for transfers between devices, on_device(): lax.all_to_all(prefix_states(got, share), 'seq', split_axis=0, concat_axi...  21.1 us
    all_to_all x1, waiting for transfers between devices, on_device(): lax.all_to_all(sent.astype(BF16).reshape(owners, CAP, -1), 'seq', split_a...  19.9 us
    unnamed x32, local copies, waits for them, and re-layouts  14.4 us
    all_to_all x1, waiting for transfers between devices, on_device(): lax.all_to_all(labels.reshape(owners, CAP), 'seq', split_axis=0, concat_a...  13.4 us
  transfers between devices with their start and end apart: 7, of which 4 were waited for; matrix products, arithmetic and copies ran while one was open for 4% of the time, Pallas kernels for 8%

profile of v1, /device:TPU:0, one launch (start us, length us, event | category | flops | bytes accessed | tf_op | source)
XLA Modules:
  0.0 504.1 jit_solution(2707155947996074133)
XLA Ops:
  7.2 0.7 all-gather.2.cloned.1.call-update
  7.9 0.9 copy_bitcast_fusion
  9.6 1.1 bitcast_multiply_fusion
  10.7 0.3 copy.56
  11.6 2.2 copy-done.1
  13.8 1.0 copy-done.7
  14.8 6.2 %local_states.1 = bf16[32,144,128]{2,1,0:T(8,128)(2,1)S(1)} custom-call(bf16[512,4096]{1,0:T(8,128)(2,1)S(1)} %copy-done.1, bf16[512,512]{1,0:T(8,128)(2,1)S(1)} %copy-done.7, f32[4,512,16]{2,1,0:T(8,128)S(1)} %bitcast.63, bf16[32,16,128]{2,1,0:T(8,128)(2,1)S(1)} %pad.5.meta_ref), custom_call_target="tpu_custom_call" | custom-call | tf_op jit(solution)/shard_map/local_states/pallas_call | solution.py:60
  21.0 49.1 %all_to_all.21.got_ref = bf16[32,144,128]{2,1,0:T(8,128)(2,1)S(1)} all-to-all(bf16[32,144,128]{2,1,0:T(8,128)(2,1)S(1)} %local_states.1), channel_id=1, replica_groups=mesh['seq'=32,'head'=1] {'seq'}, dimensions={0} | all-to-all | bytes 2359296 | tf_op jit(solution)/shard_map/all_to_all | solution.py:235
  70.4 1.0 copy-done.6
  71.4 3.0 all-to-all-start.1
  74.4 2.7 collective-permute-start
  77.1 3.6 collective-permute-start.1
  80.7 0.7 copy.51
  81.4 1.0 reshape_reshape.3
  82.4 1.3 copy.52
  83.7 0.9 convert_reduce_fusion
  84.6 1.2 multiply_add_fusion
  85.8 1.2 fusion.31
  87.1 1.3 copy.54
  88.4 0.7 broadcast_in_dim.40
  89.2 0.7 add.107
  89.9 0.8 compare_and_fusion.1
  90.7 21.1 %all-to-all-done.1.in_ref = bf16[32,128,128]{2,1,0:T(8,128)(2,1)S(1)} async-done(((bf16[32,128,128]{2,1,0:T(8,128)(2,1)}), bf16[32,128,128]{2,1,0:T(8,128)(2,1)S(1)}, u32[]{:S(2)}, u32[]{:S(2)}) %all-to-all-start.1) | async-done | bytes 1048608 | tf_op jit(solution)/shard_map/all_to_all | solution.py:236
  111.8 2.3 copy-done.2
  114.1 1.2 copy-done.4
  115.3 1.2 copy-done.5
  116.6 1.1 copy-done.8
  117.6 1.1 copy-done.9
  118.7 34.6 %mixer.1 = bf16[512,4096]{1,0:T(8,128)(2,1)S(1)} custom-call(bf16[512,4096]{1,0:T(8,128)(2,1)S(1)} %copy-done.2, bf16[512,4096]{1,0:T(8,128)(2,1)} %gate_ref.1, bf16[512,512]{1,0:T(8,128)(2,1)S(1)} %copy-done.8, bf16[512,512]{1,0:T(8,128)(2,1)S(1)} %copy-done.9, f32[4,512,16]{2,1,0:T(8,128)S(1)} %bitcast.61, f32[64,512]{1,0:T(8,128)S(1)} %bitcast.64, ...), custom_call_target="tpu_custom_call" | custom-call | tf_op jit(solution)/shard_map/mixer/pallas_call | solution.py:163
  153.3 2.0 copy-done.3
  155.3 0.7 fusion.10
  156.0 1.3 copy-done.11
  157.4 1.3 collective-permute-start.2
  158.9 0.7 sub.64
  159.6 4.3 all-to-all-start.3
  163.9 1.6 convolution_convert_fusion.1
  165.5 1.1 reshape.211
  166.6 13.4 %all-to-all-done.3 = s32[32,1,2]{2,1,0:T(1,128)S(1)} async-done(((s32[32,1,2]{2,1,0:T(1,128)}), s32[32,1,2]{2,1,0:T(1,128)S(1)}, u32[]{:S(2)}, u32[]{:S(2)}) %all-to-all-start.3) | async-done | bytes 288 | tf_op jit(solution)/shard_map/all_to_all | solution.py:277
  180.1 5.1 %all-to-all-start.2 = ((bf16[32,2,4096]{2,1,0:T(2,128)(2,1)}), bf16[32,2,4096]{2,1,0:T(2,128)(2,1)S(1)}, u32[]{:S(2)}, u32[]{:S(2)}) async-start(bf16[32,2,4096]{2,1,0:T(2,128)(2,1)} %reshape.211), calls=%async_computation.2 | async-start | bytes 1048576 | tf_op jit(solution)/shard_map/all_to_all | solution.py:274
  185.2 0.5 broadcast.63
  185.7 0.7 reduce.14
  186.7 19.9 %all-to-all-done.2 = bf16[32,2,4096]{2,1,0:T(2,128)(2,1)S(1)} async-done(((bf16[32,2,4096]{2,1,0:T(2,128)(2,1)}), bf16[32,2,4096]{2,1,0:T(2,128)(2,1)S(1)}, u32[]{:S(2)}, u32[]{:S(2)}) %all-to-all-start.2) | async-done | bytes 524320 | tf_op jit(solution)/shard_map/all_to_all | solution.py:274
  206.8 228.1 %all-gather.2.cloned.1.call-done = bf16[4096,8192]{1,0:T(8,128)(2,1)} async-done(((bf16[4096,256]{1,0:T(8,128)(2,1)}), bf16[4096,8192]{1,0:T(8,128)(2,1)}) %all-gather.2.cloned.1.call-update) | async-done | bytes 67108880 | tf_op jit(solution)/shard_map/all_gather | solution.py:207
  434.9 47.9 %convolution_convert_fusion = bf16[576,8192]{1,0:T(8,128)(2,1)} fusion(bf16[4096,8192]{1,0:T(8,128)(2,1)} %all-gather.2.cloned.1.call-done, bf16[64,4096]{1,0:T(8,128)(2,1)S(1)} %reshape.212, bf16[512,4096]{1,0:T(8,128)(2,1)} %copy-done.3), kind=kOutput, calls=%fused_computation | convolution fusion | flops 38668861440 | bytes 81264640 | tf_op jit(solution)/shard_map/dot_general | solution.py:286
  482.8 7.8 %slice.48 = bf16[512,8192]{1,0:T(8,128)(2,1)} slice(bf16[576,8192]{1,0:T(8,128)(2,1)} %convolution_convert_fusion), slice={[0:512], [0:8192]} | slice | bytes 16777216 | tf_op jit(solution)/shard_map/slice | solution.py:295
  490.6 1.8 fusion.32
  492.6 0.5 bitcast_select_fusion
  493.2 4.0 convolution_bitcast_fusion
  (54 shorter events, 2.7 us)
Async XLA Ops:
  7.2 483.5 %copy-start = (bf16[1,8192,128]{2,1,0:T(8,128)(2,1)S(1)}, bf16[1,8192,128]{2,1,0:T(8,128)(2,1)}, u32[]{:S(2)}) copy-start(bf16[1,8192,128]{2,1,0:T(8,128)(2,1)} %param.23) | copy-start | bytes 6291460
  7.2 427.7 %all-gather.2.cloned.1.call-start = ((), (), s32[]{:S(2)}) async-start(), calls=%async_computation.4 | async-start | bytes 69206016 | tf_op jit(solution)/shard_map/all_gather | solution.py:207
  11.6 2.2 copy-start.1
  13.8 1.0 copy-start.7
  21.0 66.1 %copy-start.12 = (f32[512,64]{0,1:T(8,128)S(1)}, f32[512,64]{0,1:T(8,128)}, u32[]{:S(2)}) copy-start(f32[512,64]{0,1:T(8,128)} %param.18) | copy-start | bytes 393220
  70.1 41.7 %copy-start.10 = (f32[4096]{0:T(1024)S(1)}, f32[4096]{0:T(1024)}, u32[]{:S(2)}) copy-start(f32[4096]{0:T(1024)} %param.21) | copy-start | bytes 49156
  70.4 1.0 copy-start.6
  71.4 40.4 %all-to-all-start.1 = ((bf16[32,128,128]{2,1,0:T(8,128)(2,1)}), bf16[32,128,128]{2,1,0:T(8,128)(2,1)S(1)}, u32[]{:S(2)}, u32[]{:S(2)}) async-start(bf16[32,128,128]{2,1,0:T(8,128)(2,1)} %copy-done.6), calls=%async_computation.1 | async-start | bytes 2097152 | tf_op jit(solution)/shard_map/all_to_all | solution.py:236
  74.4 14.8 %collective-permute-start = (s32[64]{0:T(128)}, s32[64]{0:T(128)}, u32[]{:S(2)}, u32[]{:S(2)}) collective-permute-start(s32[64]{0:T(128)} %param.24), channel_id=1, source_target_pairs={{0,1},{1,2},{2,3},{3,4},{4,5},{5,6},{6,7},{7,8},{8,9},{9,10},{10,1... | collective-permute-start | bytes 776 | tf_op jit(solution)/shard_map/ppermute | solution.py:23
  77.1 12.1 %collective-permute-start.1 = (s32[64]{0:T(128)}, s32[64]{0:T(128)}, u32[]{:S(2)}, u32[]{:S(2)}) collective-permute-start(s32[64]{0:T(128)} %param.25), channel_id=1, source_target_pairs={{0,1},{1,2},{2,3},{3,4},{4,5},{5,6},{6,7},{7,8},{8,9},{9,10},{10,1... | collective-permute-start | bytes 776 | tf_op jit(solution)/shard_map/ppermute | solution.py:23
  111.8 2.3 copy-start.2
  114.1 1.2 copy-start.4
  115.3 1.2 copy-start.5
  116.6 1.1 copy-start.8
  117.6 1.1 copy-start.9
  153.3 2.0 copy-start.3
  153.3 5.4 %copy-start.14 = (s32[64]{0:T(128)S(1)}, s32[64]{0:T(128)}, u32[]{:S(2)}) copy-start(s32[64]{0:T(128)} %param.27) | copy-start | bytes 772
  153.3 5.4 %copy-start.15 = (s32[64]{0:T(128)S(1)}, s32[64]{0:T(128)}, u32[]{:S(2)}) copy-start(s32[64]{0:T(128)} %multiply_add_fusion) | copy-start | bytes 772
  153.3 10.5 %copy-start.13 = (f32[64]{0:T(128)S(1)}, f32[64]{0:T(128)}, u32[]{:S(2)}) copy-start(f32[64]{0:T(128)} %get-tuple-element.18) | copy-start | bytes 772
  156.0 1.3 copy-start.11
  157.4 6.5 %collective-permute-start.2 = (bf16[64,4096]{1,0:T(8,128)(2,1)S(1)}, bf16[64,4096]{1,0:T(8,128)(2,1)S(1)}, u32[]{:S(2)}, u32[]{:S(2)}) collective-permute-start(bf16[64,4096]{1,0:T(8,128)(2,1)S(1)} %slice.66), channel_id=1, source_target_pairs={{1,0},{2,1},{3,2},{4,3},{5,4},{6,5},{7,6},{8,7},{9,8},{10,9},{11,1... | collective-permute-start | bytes 1572872 | tf_op jit(solution)/shard_map/ppermute | solution.py:23
  159.6 20.5 %all-to-all-start.3 = ((s32[32,1,2]{2,1,0:T(1,128)}), s32[32,1,2]{2,1,0:T(1,128)S(1)}, u32[]{:S(2)}, u32[]{:S(2)}) async-start(s32[32,1,2]{2,1,0:T(1,128)} %bitcast.14), calls=%async_computation.3 | async-start | bytes 32768 | tf_op jit(solution)/shard_map/all_to_all | solution.py:277
  180.1 26.5 %all-to-all-start.2 = ((bf16[32,2,4096]{2,1,0:T(2,128)(2,1)}), bf16[32,2,4096]{2,1,0:T(2,128)(2,1)S(1)}, u32[]{:S(2)}, u32[]{:S(2)}) async-start(bf16[32,2,4096]{2,1,0:T(2,128)(2,1)} %reshape.211), calls=%async_computation.2 | async-start | bytes 1048576 | tf_op jit(solution)/shard_map/all_to_all | solution.py:274
Sparse Core Ops, SparseCore 0:
  9.5 425.3 all-gather.1

commit v2 on v1

--- a/solution.py
+++ b/solution.py
@@ -282,17 +282,46 @@
     return project(jnp.concatenate([y, got_means], axis=0), weight, probe, tok, labels, valid)
 
 
+def project_kernel(tok, rows_ref, weight_ref, out_ref, feature_ref):
+    out = jnp.dot(rows_ref[...], weight_ref[...], preferred_element_type=F32)
+    out_ref[...] = out[:tok].astype(BF16)
+    feature_ref[...] = out[tok:].astype(BF16)
+
+
+def project_rows(rows, weight, tok):
+    count, inner = rows.shape
+    model = weight.shape[1]
+    width = 512
+    return pl.pallas_call(
+        functools.partial(project_kernel, tok),
+        grid=(model // width,),
+        in_specs=[
+            pl.BlockSpec((count, inner), lambda n: (0, 0)),
+            pl.BlockSpec((inner, width), lambda n: (0, n)),
+        ],
+        out_specs=[
+            pl.BlockSpec((tok, width), lambda n: (0, n)),
+            pl.BlockSpec((count - tok, width), lambda n: (0, n)),
+        ],
+        out_shape=[
+            jax.ShapeDtypeStruct((tok, model), BF16),
+            jax.ShapeDtypeStruct((count - tok, model), BF16),
+        ],
+        name="project_rows",
+        compiler_params=pltpu.CompilerParams(vmem_limit_bytes=40 * 2**20),
+    )(rows, weight)
+
+
 def project(rows, weight, probe, tok, labels, valid):
-    out = jnp.dot(rows, weight, preferred_element_type=F32)
     if lax.axis_size("head") > 1:
+        out = jnp.dot(rows, weight, preferred_element_type=F32)
         layer_out = lax.psum_scatter(
             out[:tok].astype(BF16), "head", scatter_dimension=1, tiled=True
         )
         feature = lax.psum_scatter(out[tok:], "head", scatter_dimension=1, tiled=True)
         feature = feature.astype(BF16)
     else:
-        out = out.astype(BF16)
-        layer_out, feature = out[:tok], out[tok:]
+        layer_out, feature = project_rows(rows, weight, tok)
     logits = jnp.dot(feature, probe[0], preferred_element_type=F32)
     logits = lax.psum(logits, "head")
     top = jnp.max(logits, axis=1, keepdims=True)

time: 505 us -> 494 us (0.978)
  matrix products: 56.4 us -> 6.01 us
  Pallas kernels: 41.1 us -> 85.9 us
  local copies, waits for them, and re-layouts: 32.1 us -> 26.7 us
    dot_general x1 -> x0, matrix products: 47.9 us -> none  [project(): out = jnp.dot(rows, weight, preferred_element_type=F32)]
    pallas_call x0 -> x1, Pallas kernels: none -> 44.8 us  [project_rows(): pl.pallas_call(functools.partial(project_kernel, tok), grid=(model // wid...]
    slice x1 -> x0, local copies, waits for them, and re-layouts: 7.77 us -> none  [project(): layer_out, feature = (out[:tok], out[tok:])]
    all_gather x1, waiting for transfers between devices: 228 us -> 223 us  [on_device(): weight = lax.all_gather(out_weight, 'seq', axis=1, tiled=True)]
    unnamed x32 -> x34, local copies, waits for them, and re-layouts: 14.4 us -> 16.7 us
  transfers between devices with their start and end apart: 7 -> 7, of which waited for: 4 -> 4; matrix products, arithmetic and copies ran while one was open for 4% -> 5% of each run, Pallas kernels for 8% -> 8%
where the time goes in v2:
time: 494 us; the launch traced here: 493 us
  waiting for transfers between devices  278 us (56%)
  Pallas kernels  85.9 us (17%)
  blocking collectives  49.1 us (10%)
  local copies, waits for them, and re-layouts  26.7 us (5%)
  starting transfers between devices  19.7 us (4%)
  between operations  14.4 us (3%)
  other arithmetic  12.7 us (3%)
  matrix products  6.01 us (1%)
    all_gather x1, waiting for transfers between devices, on_device(): weight = lax.all_gather(out_weight, 'seq', axis=1, tiled=True)  223 us
    all_to_all x1, blocking collectives, on_device(): got = lax.all_to_all(local, 'seq', split_axis=0, concat_axis=0, tiled=True)  49.1 us
    pallas_call x1, Pallas kernels, project_rows(): pl.pallas_call(functools.partial(project_kernel, tok), grid=(model // wid...  44.8 us
    pallas_call x1, Pallas kernels, mixer(): pl.pallas_call(functools.partial(mixer_kernel, pairs), grid=(groups, tok...  34.6 us
    all_to_all x1, waiting for transfers between devices, on_device(): lax.all_to_all(prefix_states(got, share), 'seq', split_axis=0, concat_axi...  21.1 us
    all_to_all x1, waiting for transfers between devices, on_device(): lax.all_to_all(sent.astype(BF16).reshape(owners, CAP, -1), 'seq', split_a...  20.2 us
    unnamed x34, local copies, waits for them, and re-layouts  16.7 us
    all_to_all x1, waiting for transfers between devices, on_device(): lax.all_to_all(labels.reshape(owners, CAP), 'seq', split_axis=0, concat_a...  13.5 us
  transfers between devices with their start and end apart: 7, of which 4 were waited for; matrix products, arithmetic and copies ran while one was open for 5% of the time, Pallas kernels for 8%

profile of v2, /device:TPU:0, one launch (start us, length us, event | category | flops | bytes accessed | tf_op | source)
XLA Modules:
  0.0 492.9 jit_solution(876653701596316246)
XLA Ops:
  7.2 0.7 all-gather.2.cloned.1.call-update
  7.9 0.9 copy_bitcast_fusion
  9.6 1.1 bitcast_multiply_fusion
  11.6 2.2 copy-done.3
  13.8 1.0 copy-done.8
  14.8 6.2 %local_states.1 = bf16[32,144,128]{2,1,0:T(8,128)(2,1)S(1)} custom-call(bf16[512,4096]{1,0:T(8,128)(2,1)S(1)} %copy-done.3, bf16[512,512]{1,0:T(8,128)(2,1)S(1)} %copy-done.8, f32[4,512,16]{2,1,0:T(8,128)S(1)} %bitcast.64, bf16[32,16,128]{2,1,0:T(8,128)(2,1)S(1)} %pad.5.meta_ref), custom_call_target="tpu_custom_call" | custom-call | tf_op jit(solution)/shard_map/local_states/pallas_call | solution.py:60
  21.0 49.1 %all_to_all.21.got_ref = bf16[32,144,128]{2,1,0:T(8,128)(2,1)S(1)} all-to-all(bf16[32,144,128]{2,1,0:T(8,128)(2,1)S(1)} %local_states.1), channel_id=1, replica_groups=mesh['seq'=32,'head'=1] {'seq'}, dimensions={0} | all-to-all | bytes 2359296 | tf_op jit(solution)/shard_map/all_to_all | solution.py:235
  70.4 1.0 copy-done.7
  71.4 3.0 all-to-all-start.1
  74.4 2.7 collective-permute-start
  77.1 3.5 collective-permute-start.1
  80.6 0.7 copy.51
  81.4 1.0 reshape_reshape.3
  82.3 1.3 copy.52
  83.7 0.9 convert_reduce_fusion
  84.6 1.2 multiply_add_fusion
  85.8 1.2 fusion.25
  87.0 1.3 copy.54
  88.3 0.7 broadcast_in_dim.40
  89.2 0.7 add.107
  89.9 0.8 compare_and_fusion.1
  90.7 21.1 %all-to-all-done.1.in_ref = bf16[32,128,128]{2,1,0:T(8,128)(2,1)S(1)} async-done(((bf16[32,128,128]{2,1,0:T(8,128)(2,1)}), bf16[32,128,128]{2,1,0:T(8,128)(2,1)S(1)}, u32[]{:S(2)}, u32[]{:S(2)}) %all-to-all-start.1) | async-done | bytes 1048608 | tf_op jit(solution)/shard_map/all_to_all | solution.py:236
  111.8 2.3 copy-done.4
  114.1 1.2 copy-done.5
  115.3 1.2 copy-done.6
  116.6 1.1 copy-done.9
  117.6 1.1 copy-done.10
  118.7 34.6 %mixer.1 = bf16[512,4096]{1,0:T(8,128)(2,1)S(1)} custom-call(bf16[512,4096]{1,0:T(8,128)(2,1)S(1)} %copy-done.4, bf16[512,4096]{1,0:T(8,128)(2,1)} %gate_ref.1, bf16[512,512]{1,0:T(8,128)(2,1)S(1)} %copy-done.9, bf16[512,512]{1,0:T(8,128)(2,1)S(1)} %copy-done.10, f32[4,512,16]{2,1,0:T(8,128)S(1)} %bitcast.62, f32[64,512]{1,0:T(8,128)S(1)} %bitcast.65, ...), custom_call_target="tpu_custom_call" | custom-call | tf_op jit(solution)/shard_map/mixer/pallas_call | solution.py:163
  153.4 2.0 copy-done.1
  155.3 0.7 fusion.5
  156.1 1.3 copy-done.12
  157.4 1.3 collective-permute-start.2
  158.9 0.7 sub.64
  159.6 4.3 all-to-all-start.3
  163.9 1.6 convolution_convert_fusion
  165.5 1.1 reshape.211
  166.6 13.5 %all-to-all-done.3 = s32[32,1,2]{2,1,0:T(1,128)S(1)} async-done(((s32[32,1,2]{2,1,0:T(1,128)}), s32[32,1,2]{2,1,0:T(1,128)S(1)}, u32[]{:S(2)}, u32[]{:S(2)}) %all-to-all-start.3) | async-done | bytes 288 | tf_op jit(solution)/shard_map/all_to_all | solution.py:277
  180.1 4.9 all-to-all-start.2
  185.0 0.5 broadcast.63
  185.5 0.7 reduce.14
  186.5 20.2 %all-to-all-done.2 = bf16[32,2,4096]{2,1,0:T(2,128)(2,1)S(1)} async-done(((bf16[32,2,4096]{2,1,0:T(2,128)(2,1)}), bf16[32,2,4096]{2,1,0:T(2,128)(2,1)S(1)}, u32[]{:S(2)}, u32[]{:S(2)}) %all-to-all-start.2) | async-done | bytes 524320 | tf_op jit(solution)/shard_map/all_to_all | solution.py:274
  206.9 5.0 %pad_maximum_fusion.rows_ref = bf16[576,4096]{1,0:T(8,128)(2,1)} fusion(bf16[64,4096]{1,0:T(8,128)(2,1)S(1)} %reshape.212, bf16[512,4096]{1,0:T(8,128)(2,1)} %copy-done.1), kind=kLoop, calls=%fused_computation.1 | loop fusion | flops 9437184 | bytes 9437184 | tf_op jit(solution)/shard_map/concatenate | solution.py:282
  211.9 222.9 %all-gather.2.cloned.1.call-done.weight_ref = bf16[4096,8192]{1,0:T(8,128)(2,1)} async-done(((bf16[4096,256]{1,0:T(8,128)(2,1)}), bf16[4096,8192]{1,0:T(8,128)(2,1)}) %all-gather.2.cloned.1.call-update) | async-done | bytes 67108880 | tf_op jit(solution)/shard_map/all_gather | solution.py:207
  434.8 2.3 copy-done.2
  437.2 44.8 %project_rows.1 = (bf16[512,8192]{1,0:T(8,128)(2,1)}, bf16[64,8192]{1,0:T(8,128)(2,1)S(1)}) custom-call(bf16[576,4096]{1,0:T(8,128)(2,1)S(1)} %copy-done.2, bf16[4096,8192]{1,0:T(8,128)(2,1)} %all-gather.2.cloned.1.call-done.weight_ref), custom_call_target="tpu_custom_call" | custom-call | tf_op jit(solution)/shard_map/project_rows/pallas_call | solution.py:295
  482.0 0.6 fusion.26
  482.8 0.5 bitcast_select_fusion
  483.3 2.8 convolution_bitcast_fusion
  (56 shorter events, 3.0 us)
Async XLA Ops:
  7.2 474.8 %copy-start = (bf16[1,8192,128]{2,1,0:T(8,128)(2,1)S(1)}, bf16[1,8192,128]{2,1,0:T(8,128)(2,1)}, u32[]{:S(2)}) copy-start(bf16[1,8192,128]{2,1,0:T(8,128)(2,1)} %param.23) | copy-start | bytes 6291460
  7.2 427.6 %all-gather.2.cloned.1.call-start = ((), (), s32[]{:S(2)}) async-start(), calls=%async_computation.4 | async-start | bytes 69206016 | tf_op jit(solution)/shard_map/all_gather | solution.py:207
  11.6 2.2 copy-start.3
  13.8 1.0 copy-start.8
  21.0 66.0 %copy-start.13 = (f32[512,64]{0,1:T(8,128)S(1)}, f32[512,64]{0,1:T(8,128)}, u32[]{:S(2)}) copy-start(f32[512,64]{0,1:T(8,128)} %param.18) | copy-start | bytes 393220
  70.1 41.7 %copy-start.11 = (f32[4096]{0:T(1024)S(1)}, f32[4096]{0:T(1024)}, u32[]{:S(2)}) copy-start(f32[4096]{0:T(1024)} %param.21) | copy-start | bytes 49156
  70.4 1.0 copy-start.7
  71.4 40.4 %all-to-all-start.1 = ((bf16[32,128,128]{2,1,0:T(8,128)(2,1)}), bf16[32,128,128]{2,1,0:T(8,128)(2,1)S(1)}, u32[]{:S(2)}, u32[]{:S(2)}) async-start(bf16[32,128,128]{2,1,0:T(8,128)(2,1)} %copy-done.7), calls=%async_computation.1 | async-start | bytes 2097152 | tf_op jit(solution)/shard_map/all_to_all | solution.py:236
  74.4 14.8 %collective-permute-start = (s32[64]{0:T(128)}, s32[64]{0:T(128)}, u32[]{:S(2)}, u32[]{:S(2)}) collective-permute-start(s32[64]{0:T(128)} %param.24), channel_id=1, source_target_pairs={{0,1},{1,2},{2,3},{3,4},{4,5},{5,6},{6,7},{7,8},{8,9},{9,10},{10,1... | collective-permute-start | bytes 776 | tf_op jit(solution)/shard_map/ppermute | solution.py:23
  77.1 12.0 %collective-permute-start.1 = (s32[64]{0:T(128)}, s32[64]{0:T(128)}, u32[]{:S(2)}, u32[]{:S(2)}) collective-permute-start(s32[64]{0:T(128)} %param.25), channel_id=1, source_target_pairs={{0,1},{1,2},{2,3},{3,4},{4,5},{5,6},{6,7},{7,8},{8,9},{9,10},{10,1... | collective-permute-start | bytes 776 | tf_op jit(solution)/shard_map/ppermute | solution.py:23
  111.8 2.3 copy-start.4
  114.1 1.2 copy-start.5
  115.3 1.2 copy-start.6
  116.6 1.1 copy-start.9
  117.6 1.1 copy-start.10
  153.3 2.0 copy-start.1
  153.3 5.4 %copy-start.15 = (s32[64]{0:T(128)S(1)}, s32[64]{0:T(128)}, u32[]{:S(2)}) copy-start(s32[64]{0:T(128)} %param.27) | copy-start | bytes 772
  153.3 5.4 %copy-start.16 = (s32[64]{0:T(128)S(1)}, s32[64]{0:T(128)}, u32[]{:S(2)}) copy-start(s32[64]{0:T(128)} %multiply_add_fusion) | copy-start | bytes 772
  153.3 10.5 %copy-start.14 = (f32[64]{0:T(128)S(1)}, f32[64]{0:T(128)}, u32[]{:S(2)}) copy-start(f32[64]{0:T(128)} %get-tuple-element.22) | copy-start | bytes 772
  156.0 1.3 copy-start.12
  157.4 6.4 %collective-permute-start.2 = (bf16[64,4096]{1,0:T(8,128)(2,1)S(1)}, bf16[64,4096]{1,0:T(8,128)(2,1)S(1)}, u32[]{:S(2)}, u32[]{:S(2)}) collective-permute-start(bf16[64,4096]{1,0:T(8,128)(2,1)S(1)} %slice.52), channel_id=1, source_target_pairs={{1,0},{2,1},{3,2},{4,3},{5,4},{6,5},{7,6},{8,7},{9,8},{10,9},{11,1... | collective-permute-start | bytes 1572872 | tf_op jit(solution)/shard_map/ppermute | solution.py:23
  159.6 20.5 %all-to-all-start.3 = ((s32[32,1,2]{2,1,0:T(1,128)}), s32[32,1,2]{2,1,0:T(1,128)S(1)}, u32[]{:S(2)}, u32[]{:S(2)}) async-start(s32[32,1,2]{2,1,0:T(1,128)} %bitcast.14), calls=%async_computation.3 | async-start | bytes 32768 | tf_op jit(solution)/shard_map/all_to_all | solution.py:277
  180.1 26.6 %all-to-all-start.2 = ((bf16[32,2,4096]{2,1,0:T(2,128)(2,1)}), bf16[32,2,4096]{2,1,0:T(2,128)(2,1)S(1)}, u32[]{:S(2)}, u32[]{:S(2)}) async-start(bf16[32,2,4096]{2,1,0:T(2,128)(2,1)} %reshape.211), calls=%async_computation.2 | async-start | bytes 1048576 | tf_op jit(solution)/shard_map/all_to_all | solution.py:274
  434.8 2.3 copy-start.2
Sparse Core Ops, SparseCore 0:
  9.5 425.2 all-gather.1
